TPU v7x, 32 devices: a whole 2x2x4 slice. The times are simulated.
32 devices in a mesh: grp: 4 (over y, x), row: 8 (over z, core).
Axes of the slice: x: 2, y: 2, z: 4, core: 2. Of those that a mesh axis runs over, the one named last changes fastest.
Arguments:
- t_start: bfloat16 [8192, 512], P(('row', 'grp')), may hold values from -6 to 6
- h_blocks: bfloat16 [64, 4, 8, 128, 128], P('row', 'grp'), may hold values from -0.09375 to 0.09375
- h_cols: int32 [64, 4, 8], P('row', 'grp'), may hold values from 0 to 63, as said below
- t_cols: int32 [64, 3], P(('row', 'grp')), may hold values from 0 to 3, as said below
Outputs:
- t_before: bfloat16 [8192, 512], P(('row', 'grp'))
- t_last: bfloat16 [8192, 512], P(('row', 'grp'))
Inputs may be any that keep to these rules, and one draw needn't show every extreme that they name: The 8 entries of h_cols[b, g] differ, and each names a block row c with (c // 2) % 4 == g. `t_cols`: the 3 entries of a row differ.
All inputs are finite; a program needn't handle non-finite values.
Results may differ from a plain program's by a relative error of at most 0.025.
Values may be sent and summed in bfloat16 or wider, within the bound.
A program may use at most 64 MiB of HBM per device.

v0:
```python
import functools

import jax
import jax.numpy as jnp
from jax import lax
from jax.experimental import pallas as pl
from jax.experimental.pallas import tpu as pltpu
from jax.sharding import PartitionSpec as P

BS = 128
STEPS = 3
MESH = pl.DeviceIdType.MESH
BF16 = jnp.bfloat16
F32 = jnp.float32
DENSE_BYTES = 8 << 20


def kernel(dims, t_hbm, h_hbm, hc, tc, before_ref, last_ref, *scratch):
    groups, rows, rb, cb, keeps, hrows, slots, dense = dims
    bufs = scratch[:STEPS]
    hs, hd, unp, prod, stage, landed, drow, dgrp = scratch[STEPS : STEPS + 8]
    ag_s, ag_r, fw_s, fw_r, rs_s, rs_r, dr_s, dr_r, dg_s, dg_r, local = scratch[STEPS + 8 :]
    pairs = rows // 2
    nblk = rows * rb
    g = lax.axis_index("grp")
    r = lax.axis_index("row")
    pair, core = r // 2, lax.rem(r, 2)
    sibling = pair * 2 + 1 - core
    mine = pl.ds(r * rb, rb)

    def copy(src, dst, ss, rs, row=None, grp=None):
        return pltpu.make_async_remote_copy(
            src_ref=src,
            dst_ref=dst,
            send_sem=ss,
            recv_sem=rs,
            device_id=(g if grp is None else grp, r if row is None else row),
            device_id_type=MESH,
        )

    h_copy = pltpu.make_async_copy(h_hbm.at[:, 0], hs.at[:, pl.ds(0, slots)], local.at[cb])
    h_copy.start()
    barrier = pltpu.get_barrier_semaphore()
    for k in range(1, rows):
        pl.semaphore_signal(barrier, inc=1, device_id=(g, lax.rem(r + k, rows)), device_id_type=MESH)
    for k in range(1, groups):
        pl.semaphore_signal(barrier, inc=1, device_id=(lax.rem(g + k, groups), r), device_id_type=MESH)

    t_copies = []
    for c in range(cb):
        for b in range(rb):
            one = pltpu.make_async_copy(
                t_hbm.at[pl.ds(b * BS, BS), pl.ds(c * BS, BS)],
                bufs[0].at[c, r * rb + b],
                local.at[cb + 1 + c * rb + b],
            )
            one.start()
            t_copies.append(one)
    for b in range(rb):
        total = tc[b, 0]
        for s in range(1, keeps):
            total = total + tc[b, s]
        gone = cb * (cb - 1) // 2 - total
        tile = jnp.full((16, BS), gone, jnp.int32).astype(F32).astype(BF16)
        drow[r, b] = tile
        dgrp[g, b] = tile
    for one in t_copies:
        one.wait()
    pl.semaphore_wait(barrier, rows + groups - 2)

    sends = []

    def go(one):
        one.start()
        sends.append(one)

    def gather_start(chunk, buf, c):
        own = buf.at[c, mine]
        for k in range(1, pairs):
            go(copy(own, own, ag_s.at[chunk, k], ag_r.at[chunk, k], row=lax.rem(pair + k, pairs) * 2 + core))
        go(copy(own, own, fw_s.at[chunk, 0], fw_r.at[chunk, 0], row=sibling))

    def gather_finish(chunk, buf, c):
        for k in range(1, pairs):
            src = lax.rem(pair + pairs - k, pairs)
            got = buf.at[c, pl.ds((src * 2 + core) * rb, rb)]
            copy(got, got, ag_s.at[chunk, k], ag_r.at[chunk, k], row=sibling).wait_recv()
            go(copy(got, got, fw_s.at[chunk, k], fw_r.at[chunk, k], row=sibling))
        for k in range(pairs):
            src = lax.rem(pair + pairs - k, pairs)
            got = buf.at[c, pl.ds((src * 2 + 1 - core) * rb, rb)]
            copy(got, got, fw_s.at[chunk, k], fw_r.at[chunk, k], row=sibling).wait_recv()

    for k in range(1, rows):
        go(copy(drow.at[r], drow.at[r], dr_s.at[k], dr_r.at[k], row=lax.rem(r + k, rows)))
    for k in range(1, groups):
        go(copy(dgrp.at[g], dgrp.at[g], dg_s.at[k], dg_r.at[k], grp=lax.rem(g + k, groups)))
    for c in range(2):
        gather_start(c, bufs[0], c)

    hs[:, slots] = jnp.zeros((hrows, BS, BS), BF16)
    h_copy.wait()
    if dense:

        def build(b, carry):
            for c in range(nblk):
                named = (c // rb) * (groups * rb) + g * rb + c % rb
                at = jnp.int32(slots)
                for s in range(slots):
                    at = jnp.where(hc[b, 0, s] == named, s, at)
                hd[pl.ds(pl.multiple_of(b * BS, BS), BS), c * BS : (c + 1) * BS] = hs[b, at]
            return carry

        lax.fori_loop(0, hrows, build, 0)

    def full(tile):
        return jnp.concatenate([tile] * (BS // 16), axis=0)

    def unpacked(c, gone, packed):
        zero = jnp.zeros((BS, BS), BF16)
        if c == 0:
            value = packed(0)
        elif c == cb - 1:
            value = packed(c - 1)
        else:
            value = jnp.where(gone < c, packed(c - 1), packed(c))
        return jnp.where(gone == c, zero, value)

    def multiply(c, x):
        if dense:
            right = x[...].reshape(nblk * BS, BS)
            out = jnp.dot(hd[...], right, preferred_element_type=F32)
            prod[c] = out.astype(BF16).reshape(hrows, BS, BS)
            return

        def one_row(b, carry):
            out = jnp.zeros((BS, BS), F32)
            for s in range(slots):
                named = hc[b, 0, s]
                at = named // (groups * rb) * rb + lax.rem(named, rb)
                out = out + jnp.dot(hs[b, s], x[at], preferred_element_type=F32)
            prod[c, b] = out.astype(BF16)
            return carry

        lax.fori_loop(0, hrows, one_row, 0)

    def unpack_column(c, buf):
        def one(j, carry):
            gone = full(drow[j // rb, lax.rem(j, rb)])
            unp[c, j] = unpacked(c, gone, lambda p: buf[p, j])
            return carry

        lax.fori_loop(0, nblk, one, 0)

    def scatter_start(step, p):
        def one(i, carry):
            gone = full(dgrp[i // rb, lax.rem(i, rb)])
            stage[step, p, i] = jnp.where(gone > p, prod[p, i], prod[p + 1, i])
            return carry

        lax.fori_loop(0, hrows, one, 0)
        for k in range(1, groups):
            to = lax.rem(g + k, groups)
            go(copy(
                stage.at[step, p, pl.ds(to * rb, rb)],
                landed.at[step, p, g],
                rs_s.at[step * keeps + p, k],
                rs_r.at[step * keeps + p, k],
                grp=to,
            ))

    def scatter_finish(step, p):
        for k in range(1, groups):
            got = landed.at[step, p, lax.rem(g + groups - k, groups)]
            copy(got, got, rs_s.at[step * keeps + p, k], rs_r.at[step * keeps + p, k], row=sibling).wait_recv()
        for b in range(rb):
            gone = full(drow[r, b])
            total = stage[step, p, g * rb + b].astype(F32)
            for k in range(1, groups):
                total = total + landed[step, p, lax.rem(g + k, groups), b].astype(F32)
            at = r * rb + b
            if step == 0:
                new = total
            else:
                if step == 1:
                    old = jnp.where(gone > p, bufs[0][p, at], bufs[0][p + 1, at])
                else:
                    old = bufs[step - 1][p, at]
                new = 2.0 * total - old.astype(F32)
            new = new.astype(BF16)
            if step < STEPS - 1:
                bufs[step + 1][p, at] = new
            else:
                stage[step, p, g * rb + b] = new
        if step < STEPS - 1:
            gather_start(cb + step * keeps + p, bufs[step + 1], p)

    for step in range(STEPS):
        buf = bufs[step]
        for c in range(cb):
            if step == 0:
                gather_finish(c, buf, c)
                if c + 2 < cb:
                    gather_start(c + 2, buf, c + 2)
                multiply(c, buf.at[c])
            else:
                if c < keeps:
                    gather_finish(cb + (step - 1) * keeps + c, buf, c)
                unpack_column(c, buf)
                multiply(c, unp.at[c])
            if step == 0 and c == 1:
                for k in range(1, rows):
                    got = drow.at[lax.rem(r + rows - k, rows)]
                    copy(got, got, dr_s.at[k], dr_r.at[k], row=sibling).wait_recv()
                for k in range(1, groups):
                    got = dgrp.at[lax.rem(g + groups - k, groups)]
                    copy(got, got, dg_s.at[k], dg_r.at[k], row=sibling).wait_recv()
            if c >= 1:
                scatter_start(step, c - 1)
            if c >= 2:
                scatter_finish(step, c - 2)
        scatter_finish(step, keeps - 1)

    for b in range(rb):
        gone = full(drow[r, b])
        for c in range(cb):
            here = (slice(b * BS, (b + 1) * BS), slice(c * BS, (c + 1) * BS))
            before_ref[here] = unpacked(c, gone, lambda p: bufs[STEPS - 1][p, r * rb + b])
            last_ref[here] = unpacked(c, gone, lambda p: stage[STEPS - 1, p, g * rb + b])
    for one in sends:
        one.wait_send()


def per_device(t_start, h_blocks, h_cols, t_cols):
    groups, rows = lax.axis_size("grp"), lax.axis_size("row")
    rb, cb = t_start.shape[0] // BS, t_start.shape[1] // BS
    hrows, slots = h_blocks.shape[0], h_blocks.shape[2]
    keeps = t_cols.shape[1]
    nblk = rows * rb
    pairs = rows // 2
    dense = hrows * nblk * BS * BS * 2 <= DENSE_BYTES
    chunks = cb + (STEPS - 1) * keeps
    dma = pltpu.SemaphoreType.DMA
    out = jax.ShapeDtypeStruct(t_start.shape, t_start.dtype)
    return pl.pallas_call(
        functools.partial(kernel, (groups, rows, rb, cb, keeps, hrows, slots, dense)),
        out_shape=(out, out),
        in_specs=[
            pl.BlockSpec(memory_space=pl.ANY),
            pl.BlockSpec(memory_space=pl.ANY),
            pl.BlockSpec(memory_space=pltpu.SMEM),
            pl.BlockSpec(memory_space=pltpu.SMEM),
        ],
        out_specs=(pl.BlockSpec(memory_space=pltpu.VMEM),) * 2,
        scratch_shapes=[
            pltpu.VMEM((cb, nblk, BS, BS), BF16),
            *[pltpu.VMEM((keeps, nblk, BS, BS), BF16) for _ in range(STEPS - 1)],
            pltpu.VMEM((hrows, slots + 1, BS, BS), BF16),
            pltpu.VMEM((hrows * BS, nblk * BS) if dense else (16, BS), BF16),
            pltpu.VMEM((cb, nblk, BS, BS), BF16),
            pltpu.VMEM((cb, hrows, BS, BS), BF16),
            pltpu.VMEM((STEPS, keeps, hrows, BS, BS), BF16),
            pltpu.VMEM((STEPS, keeps, groups, rb, BS, BS), BF16),
            pltpu.VMEM((rows, rb, 16, BS), BF16),
            pltpu.VMEM((groups, rb, 16, BS), BF16),
            dma((chunks, pairs)),
            dma((chunks, pairs)),
            dma((chunks, pairs)),
            dma((chunks, pairs)),
            dma((STEPS * keeps, groups)),
            dma((STEPS * keeps, groups)),
            dma((rows,)),
            dma((rows,)),
            dma((groups,)),
            dma((groups,)),
            dma((cb + 1 + cb * rb,)),
        ],
        compiler_params=pltpu.CompilerParams(
            collective_id=0, has_side_effects=True, vmem_limit_bytes=56 << 20
        ),
    )(t_start, h_blocks, h_cols, t_cols)


def solution(mesh):
    placed = (
        P(("row", "grp"), None),
        P("row", "grp", None, None, None),
        P("row", "grp", None),
        P(("row", "grp"), None),
    )
    return jax.shard_map(
        per_device,
        mesh=mesh,
        in_specs=placed,
        out_specs=(P(("row", "grp"), None), P(("row", "grp"), None)),
        check_vma=False,
    )
```

profile of v0, /device:TPU:0, one launch (start us, length us, event | category | flops | bytes accessed | tf_op | source)
XLA Modules:
  0.0 91.9 jit_solution(15069783629652526109)
XLA Ops:
  0.6 87.9 %shard_map.59 = (bf16[256,512]{1,0:T(8,128)(2,1)}, bf16[256,512]{1,0:T(8,128)(2,1)}) custom-call(bf16[256,512]{1,0:T(8,128)(2,1)} %t_hbm.1, bf16[8,1,8,128,128]{4,3,2,1,0:T(8,128)(2,1)} %h_hbm.1, s32[8,1,8]{2,1,0:T(1,128)} %hc.1, s32[2,3]{1,0:T(2,128)} %tc.1), custom_call_target="tpu_custom_call" | custom-call | tf_op jit(solution)/shard_map/pallas_call | solution.py:245
  88.6 1.7 %copy.8 = bf16[256,512]{1,0:T(8,128)(2,1)} copy(bf16[256,512]{1,0:T(8,128)(2,1)} %get-tuple-element.4) | data formatting | bytes 524288
  90.3 1.7 %copy.9 = bf16[256,512]{1,0:T(8,128)(2,1)} copy(bf16[256,512]{1,0:T(8,128)(2,1)} %get-tuple-element.5) | data formatting | bytes 524288
where the time goes:
time: 92.2 us; the launch traced here: 91.9 us
  Pallas kernels  87.9 us (95%)
  local copies, waits for them, and re-layouts  3.34 us (4%)
    pallas_call x1, Pallas kernels, per_device(): pl.pallas_call(functools.partial(kernel, (groups, rows, rb, cb, keeps, hr...  87.9 us
    unnamed x2, local copies, waits for them, and re-layouts  3.34 us

commit v1 on v0

v1 whole, which is shorter than its diff:
```python
import functools

import jax
import jax.numpy as jnp
from jax import lax
from jax.experimental import pallas as pl
from jax.experimental.pallas import tpu as pltpu
from jax.sharding import PartitionSpec as P

BS = 128
STEPS = 3
CHUNKS = 4
SUB = BS // CHUNKS
TILE = 16
MESH = pl.DeviceIdType.MESH
BF16 = jnp.bfloat16
F32 = jnp.float32
DENSE_BYTES = 8 << 20


def kernel(dims, t_hbm, h_hbm, hc, tc, before_ref, last_ref, *scratch):
    groups, rows, rb, cb, keeps, hrows, slots, dense = dims
    bufs = scratch[:STEPS]
    tv, hs, hst, hd, unp, acc, stage, landed, dgrp = scratch[STEPS : STEPS + 9]
    ag_s, ag_r, rl_s, fw_s, fw_r, rs_s, rs_r, dg_s, dg_r, local = scratch[STEPS + 9 :]
    pairs = rows // 2
    nblk = rows * rb
    full, packed = cb * SUB, keeps * SUB
    wide = rb * BS
    phases = STEPS * CHUNKS
    g = lax.axis_index("grp")
    r = lax.axis_index("row")
    pair, core = r // 2, lax.rem(r, 2)
    sibling = pair * 2 + 1 - core

    def copy(src, dst, ss, rs, row=None, grp=None):
        return pltpu.make_async_remote_copy(
            src_ref=src,
            dst_ref=dst,
            send_sem=ss,
            recv_sem=rs,
            device_id=(g if grp is None else grp, r if row is None else row),
            device_id_type=MESH,
        )

    t_copy = pltpu.make_async_copy(t_hbm, tv, local.at[0])
    t_copy.start()
    h_copy = pltpu.make_async_copy(h_hbm.at[:, 0], hs, local.at[1])
    h_copy.start()

    reach = [d for d in (2, -2, 1, -1) if abs(d) < pairs]

    def there(d):
        return (pair + d >= 0) & (pair + d < pairs)

    def at_pair(d):
        return lax.rem(pair + d + 2 * pairs, pairs) * 2 + core

    barrier = pltpu.get_barrier_semaphore()
    greeted = jnp.int32(groups)
    for k in range(1, groups):
        pl.semaphore_signal(barrier, inc=1, device_id=(lax.rem(g + k, groups), r), device_id_type=MESH)
    pl.semaphore_signal(barrier, inc=1, device_id=(g, sibling), device_id_type=MESH)
    for d in reach:

        @pl.when(there(d))
        def _():
            pl.semaphore_signal(barrier, inc=1, device_id=(g, at_pair(d)), device_id_type=MESH)

        greeted = greeted + jnp.where(there(d), 1, 0)

    lanes = []
    for b in range(rb):
        total = tc[b, 0]
        for s in range(1, keeps):
            total = total + tc[b, s]
        lanes.append(jnp.full((TILE, BS), cb * (cb - 1) // 2 - total, jnp.int32).astype(F32).astype(BF16))
    mark = jnp.concatenate(lanes, axis=1)
    dgrp[g] = mark
    bufs[0][0, r, full:, :] = mark
    t_copy.wait()
    turned = tv[...].T
    for q in range(CHUNKS):
        for c in range(cb):
            at = c * BS + q * SUB
            bufs[0][q, r, c * SUB : (c + 1) * SUB, :] = turned[at : at + SUB, :]
    pl.semaphore_wait(barrier, greeted)

    sends = [[] for _ in range(phases)]

    def go(phase, one, cond=None):
        if cond is None:
            one.start()
        else:
            pl.when(cond)(one.start)
        sends[phase].append((one, cond))

    def drain(phase):
        for one, cond in sends[phase]:
            if cond is None:
                one.wait_send()
            else:
                pl.when(cond)(one.wait_send)

    def piece(phase, who):
        step, q = divmod(phase, CHUNKS)
        if step:
            return bufs[step].at[q, who]
        return bufs[0].at[q, who] if q == 0 else bufs[0].at[q, who, pl.ds(0, full)]

    def gather_start(phase):
        own = piece(phase, r)
        for n, d in enumerate(reach):
            go(phase, copy(own, own, ag_s.at[phase, n], ag_r.at[phase, pair], row=at_pair(d)), there(d))
        go(phase, copy(own, own, fw_s.at[phase, 0], fw_r.at[phase, pair], row=sibling))

    inner = jnp.minimum(pair, pairs - 1 - pair)
    side = jnp.where(pair * 2 < pairs, 1, -1)

    def kth(k):
        both = k <= 2 * inner
        apart = jnp.where(both, (k + 1) // 2, k - inner)
        toward = jnp.where(both & (k % 2 == 1), -side, side)
        return pair + toward * apart, apart, toward

    order = [kth(k) for k in range(1, pairs)]

    for k in range(1, groups):
        go(0, copy(dgrp.at[g], dgrp.at[g], dg_s.at[k], dg_r.at[k], grp=lax.rem(g + k, groups)))
    gather_start(0)
    gather_start(1)

    h_copy.wait()
    for b in range(hrows):
        turned = hs[b].reshape(slots * BS, BS).T
        for s in range(slots):
            hst[b, s] = turned[:, s * BS : (s + 1) * BS]
        if dense:
            hst[b, slots] = jnp.zeros((BS, BS), BF16)
    if dense:
        for b in range(hrows):

            def build(c, carry):
                named = (c // rb) * (groups * rb) + g * rb + lax.rem(c, rb)
                at = jnp.int32(slots)
                for s in range(slots):
                    at = jnp.where(hc[b, 0, s] == named, s, at)
                hd[c, :, b * BS : (b + 1) * BS] = hst[b, at]
                return carry

            lax.fori_loop(0, nblk, build, 0)

    def tall(tile):
        return jnp.concatenate([tile] * (SUB // TILE), axis=0)

    def gone_of(who):
        return tall(bufs[0][0, who, full:, :])

    def part(c):
        return slice(c * SUB, (c + 1) * SUB)

    def unpacked(gone, value):
        zero = jnp.zeros((SUB, wide), BF16)
        out = []
        for c in range(cb):
            if c == 0:
                one = value(0)
            elif c == cb - 1:
                one = value(c - 1)
            else:
                one = jnp.where(gone < c, value(c - 1), value(c))
            out.append(jnp.where(gone == c, zero, one))
        return jnp.concatenate(out, axis=0)

    def operand(phase, who):
        step, q = divmod(phase, CHUNKS)
        if step == 0:
            return bufs[0][q, who, :full, :]
        return unpacked(gone_of(who), lambda p: bufs[step][q, who, part(p), :])

    def multiply(phase, src, first):
        both = [operand(phase, src * 2 + n) for n in range(2)]
        if not dense:
            for n in range(2):
                for b in range(rb):
                    unp[(src * 2 + n) * rb + b] = both[n][:, b * BS : (b + 1) * BS]
            return
        right = hd[pl.ds(src * 2 * rb, 2 * rb)].reshape(2 * wide, hrows * BS)
        out = jnp.dot(jnp.concatenate(both, axis=1), right, preferred_element_type=F32)
        for k in range(groups):
            value = out[:, k * wide : (k + 1) * wide]
            acc[k] = value if first else acc[k] + value

    def multiply_sparse():
        def one_group(k, carry):
            for b in range(rb):
                i = k * rb + b
                out = jnp.zeros((full, BS), F32)
                for s in range(slots):
                    named = hc[i, 0, s]
                    at = named // (groups * rb) * rb + lax.rem(named, rb)
                    out = out + jnp.dot(unp[at], hst[i, s], preferred_element_type=F32)
                acc[k, :, b * BS : (b + 1) * BS] = out
            return carry

        lax.fori_loop(0, groups, one_group, 0)

    def gather_multiply(phase, then=None):
        def forwarded(src):
            got = piece(phase, src * 2 + 1 - core)
            copy(got, got, fw_s.at[phase, 0], fw_r.at[phase, src], row=sibling).wait_recv()

        before = pair
        for n, (src, apart, toward) in enumerate(order):
            got = piece(phase, src * 2 + core)
            copy(got, got, fw_s.at[phase, 0], ag_r.at[phase, src], row=sibling).wait_recv()
            if n + 1 >= 2:
                go(
                    phase,
                    copy(got, got, rl_s.at[phase, n], ag_r.at[phase, src], row=lax.rem(pair - toward + pairs, pairs) * 2 + core),
                    (apart >= 2) & (pair - toward >= 0) & (pair - toward < pairs),
                )
            go(phase, copy(got, got, fw_s.at[phase, n + 1], fw_r.at[phase, src], row=sibling))
            forwarded(before)
            multiply(phase, before, n == 0)
            before = src
        if then is not None:
            then()
        forwarded(before)
        multiply(phase, before, pairs == 1)
        if not dense:
            multiply_sparse()

    def scatter_start(phase):
        for k in range(1, groups + 1):
            to = lax.rem(g + k, groups)
            gone = tall(dgrp[to])
            for p in range(keeps):
                low, high = acc[to, part(p), :].astype(BF16), acc[to, part(p + 1), :].astype(BF16)
                stage[phase, to, part(p), :] = jnp.where(gone > p, low, high)
            if k < groups:
                go(phase, copy(stage.at[phase, to], landed.at[phase, g], rs_s.at[phase, k], rs_r.at[phase, k], grp=to))

    def scatter_finish(phase):
        step, q = divmod(phase, CHUNKS)
        for k in range(1, groups):
            got = landed.at[phase, lax.rem(g + groups - k, groups)]
            copy(got, got, rs_s.at[phase, k], rs_r.at[phase, k], row=sibling).wait_recv()
        gone = tall(dgrp[g])
        for p in range(keeps):
            new = stage[phase, g, part(p), :].astype(F32)
            for k in range(1, groups):
                new = new + landed[phase, lax.rem(g + k, groups), part(p), :].astype(F32)
            if step == 1:
                old = jnp.where(gone > p, bufs[0][q, r, part(p), :], bufs[0][q, r, part(p + 1), :])
                new = 2.0 * new - old.astype(F32)
            elif step > 1:
                new = 2.0 * new - bufs[step - 1][q, r, part(p), :].astype(F32)
            if step < STEPS - 1:
                bufs[step + 1][q, r, part(p), :] = new.astype(BF16)
            else:
                stage[phase, g, part(p), :] = new.astype(BF16)
        if step < STEPS - 1:
            gather_start(phase + CHUNKS)

    def deliver(ref, source):
        gone = tall(dgrp[g])
        pieces = [unpacked(gone, lambda p: source(q, p)) for q in range(CHUNKS)]
        whole = jnp.concatenate([pieces[q][part(c), :] for c in range(cb) for q in range(CHUNKS)], axis=0)
        ref[...] = whole.T

    for phase in range(phases):
        ahead = phase + 2 if phase + 2 < CHUNKS else None
        gather_multiply(phase, None if ahead is None else functools.partial(gather_start, ahead))
        if phase == 0:
            for k in range(1, groups):
                got = dgrp.at[lax.rem(g + groups - k, groups)]
                copy(got, got, dg_s.at[k], dg_r.at[k], row=sibling).wait_recv()
        scatter_start(phase)
        if phase:
            scatter_finish(phase - 1)
        if phase >= 3:
            drain(phase - 3)
    deliver(before_ref, lambda q, p: bufs[STEPS - 1][q, r, part(p), :])
    scatter_finish(phases - 1)
    deliver(last_ref, lambda q, p: stage[(STEPS - 1) * CHUNKS + q, g, part(p), :])
    for phase in range(phases - 3, phases):
        drain(phase)


def per_device(t_start, h_blocks, h_cols, t_cols):
    groups, rows = lax.axis_size("grp"), lax.axis_size("row")
    rb, cb = t_start.shape[0] // BS, t_start.shape[1] // BS
    hrows, slots = h_blocks.shape[0], h_blocks.shape[2]
    keeps = t_cols.shape[1]
    nblk = rows * rb
    pairs = rows // 2
    wide = rb * BS
    dense = hrows * nblk * BS * BS * 2 <= DENSE_BYTES
    phases = STEPS * CHUNKS
    dma = pltpu.SemaphoreType.DMA
    out = jax.ShapeDtypeStruct(t_start.shape, t_start.dtype)
    return pl.pallas_call(
        functools.partial(kernel, (groups, rows, rb, cb, keeps, hrows, slots, dense)),
        out_shape=(out, out),
        in_specs=[
            pl.BlockSpec(memory_space=pl.ANY),
            pl.BlockSpec(memory_space=pl.ANY),
            pl.BlockSpec(memory_space=pltpu.SMEM),
            pl.BlockSpec(memory_space=pltpu.SMEM),
        ],
        out_specs=(pl.BlockSpec(memory_space=pltpu.VMEM),) * 2,
        scratch_shapes=[
            pltpu.VMEM((CHUNKS, rows, cb * SUB + TILE, wide), BF16),
            *[pltpu.VMEM((CHUNKS, rows, keeps * SUB, wide), BF16) for _ in range(STEPS - 1)],
            pltpu.VMEM(t_start.shape, BF16),
            pltpu.VMEM((hrows, slots, BS, BS), BF16),
            pltpu.VMEM((hrows, slots + 1, BS, BS), BF16),
            pltpu.VMEM((nblk, BS, hrows * BS) if dense else (1, TILE, BS), BF16),
            pltpu.VMEM((1, TILE, BS) if dense else (nblk, cb * SUB, BS), BF16),
            pltpu.VMEM((groups, cb * SUB, wide), F32),
            pltpu.VMEM((phases, groups, keeps * SUB, wide), BF16),
            pltpu.VMEM((phases, groups, keeps * SUB, wide), BF16),
            pltpu.VMEM((groups, TILE, wide), BF16),
            dma((phases, 4)),
            dma((phases, pairs)),
            dma((phases, pairs)),
            dma((phases, pairs)),
            dma((phases, pairs)),
            dma((phases, groups)),
            dma((phases, groups)),
            dma((groups,)),
            dma((groups,)),
            dma((2,)),
        ],
        compiler_params=pltpu.CompilerParams(
            collective_id=0, has_side_effects=True, vmem_limit_bytes=56 << 20
        ),
    )(t_start, h_blocks, h_cols, t_cols)


def solution(mesh):
    placed = (
        P(("row", "grp"), None),
        P("row", "grp", None, None, None),
        P("row", "grp", None),
        P(("row", "grp"), None),
    )
    return jax.shard_map(
        per_device,
        mesh=mesh,
        in_specs=placed,
        out_specs=(P(("row", "grp"), None), P(("row", "grp"), None)),
        check_vma=False,
    )
```

time: 92.2 us -> 74.8 us (0.81)
  Pallas kernels: 87.9 us -> 70.6 us
    pallas_call x1, Pallas kernels: 87.9 us -> 70.6 us  [per_device(): pl.pallas_call(functools.partial(kernel, (groups, rows, rb, cb, keeps, hr...]
where the time goes in v1:
time: 74.8 us; the launch traced here: 74.6 us
  Pallas kernels  70.6 us (94%)
  local copies, waits for them, and re-layouts  3.34 us (4%)
    pallas_call x1, Pallas kernels, per_device(): pl.pallas_call(functools.partial(kernel, (groups, rows, rb, cb, keeps, hr...  70.6 us
    unnamed x2, local copies, waits for them, and re-layouts  3.34 us

profile of v1, /device:TPU:0, one launch (start us, length us, event | category | flops | bytes accessed | tf_op | source)
XLA Modules:
  0.0 74.6 jit_solution(10769557003362124425)
XLA Ops:
  0.6 70.6 %shard_map.59 = (bf16[256,512]{1,0:T(8,128)(2,1)}, bf16[256,512]{1,0:T(8,128)(2,1)}) custom-call(bf16[256,512]{1,0:T(8,128)(2,1)} %t_hbm.1, bf16[8,1,8,128,128]{4,3,2,1,0:T(8,128)(2,1)} %h_hbm.1, s32[8,1,8]{2,1,0:T(1,128)} %hc.1, s32[2,3]{1,0:T(2,128)} %tc.1), custom_call_target="tpu_custom_call" | custom-call | tf_op jit(solution)/shard_map/pallas_call | solution.py:303
  71.2 1.7 %copy.8 = bf16[256,512]{1,0:T(8,128)(2,1)} copy(bf16[256,512]{1,0:T(8,128)(2,1)} %get-tuple-element.4) | data formatting | bytes 524288
  72.9 1.7 %copy.9 = bf16[256,512]{1,0:T(8,128)(2,1)} copy(bf16[256,512]{1,0:T(8,128)(2,1)} %get-tuple-element.5) | data formatting | bytes 524288

commit v2 on v1

--- a/solution.py
+++ b/solution.py
@@ -16,6 +16,7 @@
 BF16 = jnp.bfloat16
 F32 = jnp.float32
 DENSE_BYTES = 8 << 20
+AHEAD = 4
 
 
 def kernel(dims, t_hbm, h_hbm, hc, tc, before_ref, last_ref, *scratch):
@@ -48,10 +49,15 @@
     h_copy = pltpu.make_async_copy(h_hbm.at[:, 0], hs, local.at[1])
     h_copy.start()
 
-    reach = [d for d in (2, -2, 1, -1) if abs(d) < pairs]
+    reach = [d for d in (1, -1, 2, -2) if abs(d) < pairs]
+
+    def inside(d):
+        return (pair + d >= 0) & (pair + d < pairs)
 
     def there(d):
-        return (pair + d >= 0) & (pair + d < pairs)
+        if abs(d) == 1:
+            return inside(d)
+        return (pair + d > 0) & (pair + d < pairs - 1)
 
     def at_pair(d):
         return lax.rem(pair + d + 2 * pairs, pairs) * 2 + core
@@ -63,11 +69,11 @@
     pl.semaphore_signal(barrier, inc=1, device_id=(g, sibling), device_id_type=MESH)
     for d in reach:
 
-        @pl.when(there(d))
+        @pl.when(inside(d))
         def _():
             pl.semaphore_signal(barrier, inc=1, device_id=(g, at_pair(d)), device_id_type=MESH)
 
-        greeted = greeted + jnp.where(there(d), 1, 0)
+        greeted = greeted + jnp.where(inside(d), 1, 0)
 
     lanes = []
     for b in range(rb):
@@ -127,28 +133,29 @@
 
     for k in range(1, groups):
         go(0, copy(dgrp.at[g], dgrp.at[g], dg_s.at[k], dg_r.at[k], grp=lax.rem(g + k, groups)))
-    gather_start(0)
-    gather_start(1)
-
-    h_copy.wait()
-    for b in range(hrows):
-        turned = hs[b].reshape(slots * BS, BS).T
-        for s in range(slots):
-            hst[b, s] = turned[:, s * BS : (s + 1) * BS]
-        if dense:
-            hst[b, slots] = jnp.zeros((BS, BS), BF16)
-    if dense:
+    for q in range(AHEAD):
+        gather_start(q)
+
+    def turn_blocks():
+        h_copy.wait()
         for b in range(hrows):
-
-            def build(c, carry):
-                named = (c // rb) * (groups * rb) + g * rb + lax.rem(c, rb)
+            turned = hs[b].reshape(slots * BS, BS).T
+            for s in range(slots):
+                hst[b, s] = turned[:, s * BS : (s + 1) * BS]
+            if dense:
+                hst[b, slots] = jnp.zeros((BS, BS), BF16)
+
+    def lay_out():
+        def build(c, carry):
+            named = (c // rb) * (groups * rb) + g * rb + lax.rem(c, rb)
+            for b in range(hrows):
                 at = jnp.int32(slots)
                 for s in range(slots):
                     at = jnp.where(hc[b, 0, s] == named, s, at)
                 hd[c, :, b * BS : (b + 1) * BS] = hst[b, at]
-                return carry
-
-            lax.fori_loop(0, nblk, build, 0)
+            return carry
+
+        lax.fori_loop(0, nblk, build, 0)
 
     def tall(tile):
         return jnp.concatenate([tile] * (SUB // TILE), axis=0)
@@ -205,28 +212,33 @@
 
         lax.fori_loop(0, groups, one_group, 0)
 
-    def gather_multiply(phase, then=None):
-        def forwarded(src):
-            got = piece(phase, src * 2 + 1 - core)
-            copy(got, got, fw_s.at[phase, 0], fw_r.at[phase, src], row=sibling).wait_recv()
-
+    def forwarded(phase, src):
+        got = piece(phase, src * 2 + 1 - core)
+        copy(got, got, fw_s.at[phase, 0], fw_r.at[phase, src], row=sibling).wait_recv()
+
+    def pass_on(phase, n):
+        src, apart, toward = order[n]
+        got = piece(phase, src * 2 + core)
+        copy(got, got, fw_s.at[phase, 0], ag_r.at[phase, src], row=sibling).wait_recv()
+        beyond = pair - toward
+        go(
+            phase,
+            copy(got, got, rl_s.at[phase, n], ag_r.at[phase, src], row=lax.rem(beyond + pairs, pairs) * 2 + core),
+            ((apart >= 2) | (beyond == 0) | (beyond == pairs - 1)) & (beyond >= 0) & (beyond < pairs),
+        )
+        go(phase, copy(got, got, fw_s.at[phase, n + 1], fw_r.at[phase, src], row=sibling))
+
+    def gather_multiply(phase, done=0, then=None):
         before = pair
-        for n, (src, apart, toward) in enumerate(order):
-            got = piece(phase, src * 2 + core)
-            copy(got, got, fw_s.at[phase, 0], ag_r.at[phase, src], row=sibling).wait_recv()
-            if n + 1 >= 2:
-                go(
-                    phase,
-                    copy(got, got, rl_s.at[phase, n], ag_r.at[phase, src], row=lax.rem(pair - toward + pairs, pairs) * 2 + core),
-                    (apart >= 2) & (pair - toward >= 0) & (pair - toward < pairs),
-                )
-            go(phase, copy(got, got, fw_s.at[phase, n + 1], fw_r.at[phase, src], row=sibling))
-            forwarded(before)
+        for n, (src, _, _) in enumerate(order):
+            if n >= done:
+                pass_on(phase, n)
+            forwarded(phase, before)
             multiply(phase, before, n == 0)
             before = src
         if then is not None:
             then()
-        forwarded(before)
+        forwarded(phase, before)
         multiply(phase, before, pairs == 1)
         if not dense:
             multiply_sparse()
@@ -269,14 +281,23 @@
         whole = jnp.concatenate([pieces[q][part(c), :] for c in range(cb) for q in range(CHUNKS)], axis=0)
         ref[...] = whole.T
 
+    turn_blocks()
+    early = min(2, len(order))
+    for n in range(early):
+        pass_on(0, n)
+    if dense:
+        lay_out()
     for phase in range(phases):
-        ahead = phase + 2 if phase + 2 < CHUNKS else None
-        gather_multiply(phase, None if ahead is None else functools.partial(gather_start, ahead))
+        ahead = phase + AHEAD if phase + AHEAD < CHUNKS else None
+        gather_multiply(phase, early, None if ahead is None else functools.partial(gather_start, ahead))
         if phase == 0:
             for k in range(1, groups):
                 got = dgrp.at[lax.rem(g + groups - k, groups)]
                 copy(got, got, dg_s.at[k], dg_r.at[k], row=sibling).wait_recv()
         scatter_start(phase)
+        if phase + 1 < phases and True:
+            for n in range(early):
+                pass_on(phase + 1, n)
         if phase:
             scatter_finish(phase - 1)
         if phase >= 3:
@@ -299,7 +320,7 @@
     dense = hrows * nblk * BS * BS * 2 <= DENSE_BYTES
     phases = STEPS * CHUNKS
     dma = pltpu.SemaphoreType.DMA
-    out = jax.ShapeDtypeStruct(t_start.shape, t_start.dtype)
+    out = pltpu.VMEM(t_start.shape, t_start.dtype)
     return pl.pallas_call(
         functools.partial(kernel, (groups, rows, rb, cb, keeps, hrows, slots, dense)),
         out_shape=(out, out),

time: 74.8 us -> 65.9 us (0.88)
  Pallas kernels: 70.6 us -> 63.7 us
  local copies, waits for them, and re-layouts: 3.34 us -> 1.41 us
    pallas_call x1, Pallas kernels: 70.6 us -> 63.7 us  [per_device(): pl.pallas_call(functools.partial(kernel, (groups, rows, rb, cb, keeps, hr...]
    unnamed x2, local copies, waits for them, and re-layouts: 3.34 us -> 1.41 us
where the time goes in v2:
time: 65.9 us; the launch traced here: 65.7 us
  Pallas kernels  63.7 us (97%)
  local copies, waits for them, and re-layouts  1.41 us (2%)
    pallas_call x1, Pallas kernels, per_device(): pl.pallas_call(functools.partial(kernel, (groups, rows, rb, cb, keeps, hr...  63.7 us
    unnamed x2, local copies, waits for them, and re-layouts  1.41 us

profile of v2, /device:TPU:0, one launch (start us, length us, event | category | flops | bytes accessed | tf_op | source)
XLA Modules:
  0.0 65.7 jit_solution(18292499276748884152)
XLA Ops:
  0.6 63.7 %shard_map.59 = (bf16[256,512]{1,0:T(8,128)(2,1)S(1)}, bf16[256,512]{1,0:T(8,128)(2,1)S(1)}) custom-call(bf16[256,512]{1,0:T(8,128)(2,1)} %t_hbm.1, bf16[8,1,8,128,128]{4,3,2,1,0:T(8,128)(2,1)} %h_hbm.1, s32[8,1,8]{2,1,0:T(1,128)} %hc.1, s32[2,3]{1,0:T(2,128)} %tc.1), custom_call_target="tpu_custom_call" | custom-call | tf_op jit(solution)/shard_map/pallas_call | solution.py:324
  64.3 0.7 %copy.8 = bf16[256,512]{1,0:T(8,128)(2,1)} copy(bf16[256,512]{1,0:T(8,128)(2,1)S(1)} %get-tuple-element.2) | data formatting | bytes 524288
  65.0 0.7 %copy.9 = bf16[256,512]{1,0:T(8,128)(2,1)} copy(bf16[256,512]{1,0:T(8,128)(2,1)S(1)} %get-tuple-element.3) | data formatting | bytes 524288

commit v3 on v2

v3 whole, which is shorter than its diff:
```python
import functools

import jax
import jax.numpy as jnp
from jax import lax
from jax.experimental import pallas as pl
from jax.experimental.pallas import tpu as pltpu
from jax.sharding import PartitionSpec as P

BS = 128
STEPS = 3
SIZES = (32, 32, 32, 32)
CHUNKS = len(SIZES)
FROM = tuple(sum(SIZES[:q]) for q in range(CHUNKS))
WIDEST = max(SIZES)
TILE = 16
MESH = pl.DeviceIdType.MESH
BF16 = jnp.bfloat16
F32 = jnp.float32
DENSE_BYTES = 8 << 20
AHEAD = 3


def kernel(dims, t_hbm, h_hbm, hc_hbm, tc_hbm, before_ref, last_ref, *scratch):
    groups, rows, rb, cb, keeps, hrows, slots, dense = dims
    bufs = scratch[:STEPS]
    tv, hs, hst, hd, unp, acc, stage, landed, dgrp, hc, tc = scratch[STEPS : STEPS + 11]
    ag_s, ag_r, rl_s, fw_s, fw_r, rs_s, rs_r, dg_s, dg_r, local = scratch[STEPS + 11 :]
    pairs = rows // 2
    nblk = rows * rb
    full = [cb * size for size in SIZES]
    packed = [keeps * size for size in SIZES]
    wide = rb * BS
    phases = STEPS * CHUNKS
    g = lax.axis_index("grp")
    r = lax.axis_index("row")
    pair, core = r // 2, lax.rem(r, 2)
    sibling = pair * 2 + 1 - core

    def part(q, c):
        return slice(c * SIZES[q], (c + 1) * SIZES[q])

    def copy(src, dst, ss, rs, row=None, grp=None):
        return pltpu.make_async_remote_copy(
            src_ref=src,
            dst_ref=dst,
            send_sem=ss,
            recv_sem=rs,
            device_id=(g if grp is None else grp, r if row is None else row),
            device_id_type=MESH,
        )

    t_copy = pltpu.make_async_copy(t_hbm, tv, local.at[0])
    t_copy.start()
    tc_copy = pltpu.make_async_copy(tc_hbm, tc, local.at[1])
    tc_copy.start()
    reach = [d for d in (2, -2, 1, -1) if abs(d) < pairs]

    def inside(d):
        return (pair + d >= 0) & (pair + d < pairs)

    def partner(k):
        other = g
        for i in range(groups.bit_length() - 1):
            if k >> i & 1:
                other = other + (1 - 2 * lax.rem(g // (1 << i), 2)) * (1 << i)
        return other

    def there(d):
        if abs(d) == 1:
            return inside(d)
        return (pair + d > 0) & (pair + d < pairs - 1)

    def at_pair(d):
        return lax.rem(pair + d + 2 * pairs, pairs) * 2 + core

    barrier = pltpu.get_barrier_semaphore()
    greeted = jnp.int32(groups)
    for k in range(1, groups):
        pl.semaphore_signal(barrier, inc=1, device_id=(partner(k), r), device_id_type=MESH)
    pl.semaphore_signal(barrier, inc=1, device_id=(g, sibling), device_id_type=MESH)
    for d in reach:

        @pl.when(inside(d))
        def _():
            pl.semaphore_signal(barrier, inc=1, device_id=(g, at_pair(d)), device_id_type=MESH)

        greeted = greeted + jnp.where(inside(d), 1, 0)

    h_copy = pltpu.make_async_copy(h_hbm.at[:, 0], hs, local.at[2])
    h_copy.start()
    hc_copy = pltpu.make_async_copy(hc_hbm, hc, local.at[3])
    hc_copy.start()
    tc_copy.wait()
    lanes = []
    for b in range(rb):
        total = tc[b, 0]
        for s in range(1, keeps):
            total = total + tc[b, s]
        lanes.append(jnp.full((TILE, BS), cb * (cb - 1) // 2 - total, jnp.int32).astype(F32).astype(BF16))
    mark = jnp.concatenate(lanes, axis=1)
    dgrp[g] = mark
    bufs[0][0, r, full[0] : full[0] + TILE, :] = mark
    t_copy.wait()
    turned = tv[...].T
    for q in range(CHUNKS):
        for c in range(cb):
            at = c * BS + FROM[q]
            bufs[0][q, r, part(q, c), :] = turned[at : at + SIZES[q], :]
    pl.semaphore_wait(barrier, greeted)

    sends = [[] for _ in range(phases)]

    def go(phase, one, cond=None):
        if cond is None:
            one.start()
        else:
            pl.when(cond)(one.start)
        sends[phase].append((one, cond))

    def drain(phase):
        for one, cond in sends[phase]:
            if cond is None:
                one.wait_send()
            else:
                pl.when(cond)(one.wait_send)

    def piece(phase, who):
        step, q = divmod(phase, CHUNKS)
        if step:
            return bufs[step].at[q, who, pl.ds(0, packed[q])]
        return bufs[0].at[q, who, pl.ds(0, full[q] + (0 if q else TILE))]

    def gather_start(phase):
        own = piece(phase, r)
        for n, d in enumerate(reach):
            go(phase, copy(own, own, ag_s.at[phase, n], ag_r.at[phase, pair], row=at_pair(d)), there(d))
        go(phase, copy(own, own, fw_s.at[phase, 0], fw_r.at[phase, pair], row=sibling))

    def ranked(p):
        far = 1 if 2 * p < pairs else -1
        short = lambda s: pairs == 4 and (s - p) * far < 0
        return sorted((s for s in range(pairs) if s != p), key=lambda s: (short(s), abs(s - p), (s - p) * far < 0))

    def kth(n):
        src = jnp.int32(ranked(0)[n])
        for p in range(1, pairs):
            src = jnp.where(pair == p, ranked(p)[n], src)
        toward = jnp.where(src > pair, 1, -1)
        return src, (src - pair) * toward, toward

    order = [kth(n) for n in range(pairs - 1)]

    for k in range(1, groups):
        go(0, copy(dgrp.at[g], dgrp.at[g], dg_s.at[k], dg_r.at[k], grp=partner(k)))
    for q in range(AHEAD):
        gather_start(q)

    def turn_blocks():
        h_copy.wait()
        hc_copy.wait()
        for b in range(hrows):
            turned = hs[b].reshape(slots * BS, BS).T
            for s in range(slots):
                hst[b, s] = turned[:, s * BS : (s + 1) * BS]
            if dense:
                hst[b, slots] = jnp.zeros((BS, BS), BF16)

    def lay_out():
        def build(c, carry):
            named = (c // rb) * (groups * rb) + g * rb + lax.rem(c, rb)
            for b in range(hrows):
                at = jnp.int32(slots)
                for s in range(slots):
                    at = jnp.where(hc[b, 0, s] == named, s, at)
                hd[c, :, b * BS : (b + 1) * BS] = hst[b, at]
            return carry

        lax.fori_loop(0, nblk, build, 0)

    def tall(q, tile):
        return jnp.concatenate([tile] * (SIZES[q] // TILE), axis=0)

    def gone_of(q, who):
        return tall(q, bufs[0][0, who, full[0] : full[0] + TILE, :])

    def unpacked(gone, value):
        zero = jnp.zeros(gone.shape, BF16)
        out = []
        for c in range(cb):
            if c == 0:
                one = value(0)
            elif c == cb - 1:
                one = value(c - 1)
            else:
                one = jnp.where(gone < c, value(c - 1), value(c))
            out.append(jnp.where(gone == c, zero, one))
        return jnp.concatenate(out, axis=0)

    def operand(phase, who):
        step, q = divmod(phase, CHUNKS)
        if step == 0:
            return bufs[0][q, who, : full[q], :]
        return unpacked(gone_of(q, who), lambda p: bufs[step][q, who, part(q, p), :])

    def multiply(phase, src, first):
        both = [operand(phase, src * 2 + n) for n in range(2)]
        high = full[phase % CHUNKS]
        if not dense:
            for n in range(2):
                for b in range(rb):
                    unp[(src * 2 + n) * rb + b, :high] = both[n][:, b * BS : (b + 1) * BS]
            return
        right = hd[pl.ds(src * 2 * rb, 2 * rb)].reshape(2 * wide, hrows * BS)
        out = jnp.dot(jnp.concatenate(both, axis=1), right, preferred_element_type=F32)
        for k in range(groups):
            value = out[:, k * wide : (k + 1) * wide]
            acc[k, :high] = value if first else acc[k, :high] + value

    def multiply_sparse(phase):
        high = full[phase % CHUNKS]

        def one_group(k, carry):
            for b in range(rb):
                i = k * rb + b
                out = jnp.zeros((high, BS), F32)
                for s in range(slots):
                    named = hc[i, 0, s]
                    at = named // (groups * rb) * rb + lax.rem(named, rb)
                    out = out + jnp.dot(unp[at][:high], hst[i, s], preferred_element_type=F32)
                acc[k, :high, b * BS : (b + 1) * BS] = out
            return carry

        lax.fori_loop(0, groups, one_group, 0)

    def forwarded(phase, src):
        got = piece(phase, src * 2 + 1 - core)
        copy(got, got, fw_s.at[phase, 0], fw_r.at[phase, src], row=sibling).wait_recv()

    def pass_on(phase, n):
        src, apart, toward = order[n]
        got = piece(phase, src * 2 + core)
        copy(got, got, fw_s.at[phase, 0], ag_r.at[phase, src], row=sibling).wait_recv()
        beyond = pair - toward
        go(
            phase,
            copy(got, got, rl_s.at[phase, n], ag_r.at[phase, src], row=lax.rem(beyond + pairs, pairs) * 2 + core),
            ((apart >= 2) | (beyond == 0) | (beyond == pairs - 1)) & (beyond >= 0) & (beyond < pairs),
        )
        go(phase, copy(got, got, fw_s.at[phase, n + 1], fw_r.at[phase, src], row=sibling))

    def gather_multiply(phase, done):
        before = pair
        for n, (src, _, _) in enumerate(order):
            if n >= done:
                pass_on(phase, n)
            forwarded(phase, before)
            multiply(phase, before, n == 0)
            before = src
        forwarded(phase, before)
        multiply(phase, before, pairs == 1)
        if not dense:
            multiply_sparse(phase)

    def scatter_start(phase):
        q = phase % CHUNKS
        rows_here = pl.ds(0, packed[q])
        for k in [*range(groups - 1, 0, -1), 0]:
            to = partner(k)
            gone = tall(q, dgrp[to])
            for p in range(keeps):
                low, high = acc[to, part(q, p), :].astype(BF16), acc[to, part(q, p + 1), :].astype(BF16)
                stage[phase, to, part(q, p), :] = jnp.where(gone > p, low, high)
            if k:
                go(phase, copy(stage.at[phase, to, rows_here], landed.at[phase, g, rows_here], rs_s.at[phase, k], rs_r.at[phase, k], grp=to))

    def scatter_finish(phase):
        step, q = divmod(phase, CHUNKS)
        for k in range(1, groups):
            got = landed.at[phase, partner(k), pl.ds(0, packed[q])]
            copy(got, got, rs_s.at[phase, k], rs_r.at[phase, k], row=sibling).wait_recv()
        gone = tall(q, dgrp[g])
        for p in range(keeps):
            new = stage[phase, g, part(q, p), :].astype(F32)
            for k in range(1, groups):
                new = new + landed[phase, partner(k), part(q, p), :].astype(F32)
            if step == 1:
                old = jnp.where(gone > p, bufs[0][q, r, part(q, p), :], bufs[0][q, r, part(q, p + 1), :])
                new = 2.0 * new - old.astype(F32)
            elif step > 1:
                new = 2.0 * new - bufs[step - 1][q, r, part(q, p), :].astype(F32)
            if step < STEPS - 1:
                bufs[step + 1][q, r, part(q, p), :] = new.astype(BF16)
            else:
                stage[phase, g, part(q, p), :] = new.astype(BF16)
        if step < STEPS - 1:
            gather_start(phase + CHUNKS)

    def deliver(ref, source):
        pieces = [unpacked(tall(q, dgrp[g]), functools.partial(source, q)) for q in range(CHUNKS)]
        whole = jnp.concatenate([pieces[q][part(q, c), :] for c in range(cb) for q in range(CHUNKS)], axis=0)
        ref[...] = whole.T

    turn_blocks()
    early = min(2, len(order))
    for n in range(early):
        pass_on(0, n)
    for q in range(AHEAD, CHUNKS):
        gather_start(q)
    if dense:
        lay_out()
    for phase in range(phases):
        gather_multiply(phase, early)
        if phase == 0:
            for k in range(1, groups):
                got = dgrp.at[partner(k)]
                copy(got, got, dg_s.at[k], dg_r.at[k], row=sibling).wait_recv()
        scatter_start(phase)
        if phase + 1 < phases:
            for n in range(early):
                pass_on(phase + 1, n)
        if phase:
            scatter_finish(phase - 1)
        if phase >= 3:
            drain(phase - 3)
    deliver(before_ref, lambda q, p: bufs[STEPS - 1][q, r, part(q, p), :])
    scatter_finish(phases - 1)
    deliver(last_ref, lambda q, p: stage[(STEPS - 1) * CHUNKS + q, g, part(q, p), :])
    for phase in range(phases - 3, phases):
        drain(phase)


def per_device(t_start, h_blocks, h_cols, t_cols):
    groups, rows = lax.axis_size("grp"), lax.axis_size("row")
    rb, cb = t_start.shape[0] // BS, t_start.shape[1] // BS
    hrows, slots = h_blocks.shape[0], h_blocks.shape[2]
    keeps = t_cols.shape[1]
    nblk = rows * rb
    pairs = rows // 2
    wide = rb * BS
    dense = hrows * nblk * BS * BS * 2 <= DENSE_BYTES
    phases = STEPS * CHUNKS
    dma = pltpu.SemaphoreType.DMA
    out = pltpu.VMEM(t_start.shape, t_start.dtype)
    return pl.pallas_call(
        functools.partial(kernel, (groups, rows, rb, cb, keeps, hrows, slots, dense)),
        out_shape=(out, out),
        in_specs=[
            pl.BlockSpec(memory_space=pl.ANY),
            pl.BlockSpec(memory_space=pl.ANY),
            pl.BlockSpec(memory_space=pl.ANY),
            pl.BlockSpec(memory_space=pl.ANY),
        ],
        out_specs=(pl.BlockSpec(memory_space=pltpu.VMEM),) * 2,
        scratch_shapes=[
            pltpu.VMEM((CHUNKS, rows, cb * WIDEST + TILE, wide), BF16),
            *[pltpu.VMEM((CHUNKS, rows, keeps * WIDEST, wide), BF16) for _ in range(STEPS - 1)],
            pltpu.VMEM(t_start.shape, BF16),
            pltpu.VMEM((hrows, slots, BS, BS), BF16),
            pltpu.VMEM((hrows, slots + 1, BS, BS), BF16),
            pltpu.VMEM((nblk, BS, hrows * BS) if dense else (1, TILE, BS), BF16),
            pltpu.VMEM((1, TILE, BS) if dense else (nblk, cb * WIDEST, BS), BF16),
            pltpu.VMEM((groups, cb * WIDEST, wide), F32),
            pltpu.VMEM((phases, groups, keeps * WIDEST, wide), BF16),
            pltpu.VMEM((phases, groups, keeps * WIDEST, wide), BF16),
            pltpu.VMEM((groups, TILE, wide), BF16),
            pltpu.SMEM(h_cols.shape, jnp.int32),
            pltpu.SMEM(t_cols.shape, jnp.int32),
            dma((phases, 4)),
            dma((phases, pairs)),
            dma((phases, pairs)),
            dma((phases, pairs)),
            dma((phases, pairs)),
            dma((phases, groups)),
            dma((phases, groups)),
            dma((groups,)),
            dma((groups,)),
            dma((4,)),
        ],
        compiler_params=pltpu.CompilerParams(
            collective_id=0, has_side_effects=True, vmem_limit_bytes=56 << 20
        ),
    )(t_start, h_blocks, h_cols, t_cols)


def solution(mesh):
    placed = (
        P(("row", "grp"), None),
        P("row", "grp", None, None, None),
        P("row", "grp", None),
        P(("row", "grp"), None),
    )
    return jax.shard_map(
        per_device,
        mesh=mesh,
        in_specs=placed,
        out_specs=(P(("row", "grp"), None), P(("row", "grp"), None)),
        check_vma=False,
    )
```

time: 65.9 us -> 62.5 us (0.948)
  Pallas kernels: 63.7 us -> 60.3 us
    pallas_call x1, Pallas kernels: 63.7 us -> 60.3 us  [per_device(): pl.pallas_call(functools.partial(kernel, (groups, rows, rb, cb, keeps, hr...]
where the time goes in v3:
time: 62.5 us; the launch traced here: 62.3 us
  Pallas kernels  60.3 us (96%)
  local copies, waits for them, and re-layouts  1.41 us (2%)
  between operations  0.64 us (1%)
    pallas_call x1, Pallas kernels, per_device(): pl.pallas_call(functools.partial(kernel, (groups, rows, rb, cb, keeps, hr...  60.3 us
    unnamed x2, local copies, waits for them, and re-layouts  1.41 us

profile of v3, /device:TPU:0, one launch (start us, length us, event | category | flops | bytes accessed | tf_op | source)
XLA Modules:
  0.0 62.3 jit_solution(1984462038369449139)
XLA Ops:
  0.6 60.3 %shard_map.59 = (bf16[256,512]{1,0:T(8,128)(2,1)S(1)}, bf16[256,512]{1,0:T(8,128)(2,1)S(1)}) custom-call(bf16[256,512]{1,0:T(8,128)(2,1)} %t_hbm.1, bf16[8,1,8,128,128]{4,3,2,1,0:T(8,128)(2,1)} %h_hbm.1, s32[8,1,8]{2,1,0:T(1,128)} %hc_hbm.1, s32[2,3]{1,0:T(2,128)} %tc_hbm.1), custom_call_target="tpu_custom_call" | custom-call | tf_op jit(solution)/shard_map/pallas_call | solution.py:345
  60.9 0.7 %copy.8 = bf16[256,512]{1,0:T(8,128)(2,1)} copy(bf16[256,512]{1,0:T(8,128)(2,1)S(1)} %get-tuple-element.2) | data formatting | bytes 524288
  61.6 0.7 %copy.9 = bf16[256,512]{1,0:T(8,128)(2,1)} copy(bf16[256,512]{1,0:T(8,128)(2,1)S(1)} %get-tuple-element.3) | data formatting | bytes 524288

commit v4 on v3

--- a/solution.py
+++ b/solution.py
@@ -25,7 +25,7 @@
     groups, rows, rb, cb, keeps, hrows, slots, dense = dims
     bufs = scratch[:STEPS]
     tv, hs, hst, hd, unp, acc, stage, landed, dgrp, hc, tc = scratch[STEPS : STEPS + 11]
-    ag_s, ag_r, rl_s, fw_s, fw_r, rs_s, rs_r, dg_s, dg_r, local = scratch[STEPS + 11 :]
+    ag_s, rl_s, rs_s, rs_r, ag_r, fw_r, dg_s, dg_r, local = scratch[STEPS + 11 :]
     pairs = rows // 2
     nblk = rows * rb
     full = [cb * size for size in SIZES]
@@ -109,21 +109,11 @@
             bufs[0][q, r, part(q, c), :] = turned[at : at + SIZES[q], :]
     pl.semaphore_wait(barrier, greeted)
 
-    sends = [[] for _ in range(phases)]
-
-    def go(phase, one, cond=None):
+    def go(one, cond=None):
         if cond is None:
             one.start()
         else:
             pl.when(cond)(one.start)
-        sends[phase].append((one, cond))
-
-    def drain(phase):
-        for one, cond in sends[phase]:
-            if cond is None:
-                one.wait_send()
-            else:
-                pl.when(cond)(one.wait_send)
 
     def piece(phase, who):
         step, q = divmod(phase, CHUNKS)
@@ -133,9 +123,9 @@
 
     def gather_start(phase):
         own = piece(phase, r)
-        for n, d in enumerate(reach):
-            go(phase, copy(own, own, ag_s.at[phase, n], ag_r.at[phase, pair], row=at_pair(d)), there(d))
-        go(phase, copy(own, own, fw_s.at[phase, 0], fw_r.at[phase, pair], row=sibling))
+        for d in reach:
+            go(copy(own, own, ag_s.at[phase], ag_r.at[phase, pair], row=at_pair(d)), there(d))
+        go(copy(own, own, ag_s.at[phase], fw_r.at[phase, pair], row=sibling))
 
     def ranked(p):
         far = 1 if 2 * p < pairs else -1
@@ -152,7 +142,7 @@
     order = [kth(n) for n in range(pairs - 1)]
 
     for k in range(1, groups):
-        go(0, copy(dgrp.at[g], dgrp.at[g], dg_s.at[k], dg_r.at[k], grp=partner(k)))
+        go(copy(dgrp.at[g], dgrp.at[g], dg_s.at[k], dg_r.at[k], grp=partner(k)))
     for q in range(AHEAD):
         gather_start(q)
 
@@ -202,6 +192,19 @@
         if step == 0:
             return bufs[0][q, who, : full[q], :]
         return unpacked(gone_of(q, who), lambda p: bufs[step][q, who, part(q, p), :])
+
+    def multiply_half(phase, who, first):
+        high = full[phase % CHUNKS]
+        if not dense:
+            one = operand(phase, who)
+            for b in range(rb):
+                unp[who * rb + b, :high] = one[:, b * BS : (b + 1) * BS]
+            return
+        right = hd[pl.ds(who * rb, rb)].reshape(wide, hrows * BS)
+        out = jnp.dot(operand(phase, who), right, preferred_element_type=F32)
+        for k in range(groups):
+            value = out[:, k * wide : (k + 1) * wide]
+            acc[k, :high] = value if first else acc[k, :high] + value
 
     def multiply(phase, src, first):
         both = [operand(phase, src * 2 + n) for n in range(2)]
@@ -235,19 +238,46 @@
 
     def forwarded(phase, src):
         got = piece(phase, src * 2 + 1 - core)
-        copy(got, got, fw_s.at[phase, 0], fw_r.at[phase, src], row=sibling).wait_recv()
+        copy(got, got, ag_s.at[phase], fw_r.at[phase, src], row=sibling).wait_recv()
+
+    def relayed(src, apart, toward):
+        beyond = pair - toward
+        return ((apart >= 2) | (beyond == 0) | (beyond == pairs - 1)) & (beyond >= 0) & (beyond < pairs)
+
+    def total(conds):
+        return sum(jnp.where(cond, 1, 0) for cond in conds)
+
+    sent = total(there(d) for d in reach) + pairs
+    passed = total(relayed(*one) for one in order)
+
+    def drain(phase):
+        step, q = divmod(phase, CHUNKS)
+        high = packed[q] if step else full[q] + (0 if q else TILE)
+
+        def settle(sem, count, choices):
+            for n in choices:
+
+                @pl.when(count == n)
+                def _():
+                    some = bufs[step].at[q, pl.ds(0, n), pl.ds(0, high)]
+                    copy(some, some, sem.at[phase], sem.at[phase], row=sibling).wait_send()
+
+        few = pairs == 4
+        settle(ag_s, sent, [pairs + 2] if few else range(pairs, pairs + 5))
+        settle(rl_s, passed, [2] if few else range(1, pairs))
+        some = stage.at[phase, pl.ds(0, groups - 1), pl.ds(0, packed[q])]
+        copy(some, some, rs_s.at[phase], rs_s.at[phase], row=sibling).wait_send()
 
     def pass_on(phase, n):
         src, apart, toward = order[n]
         got = piece(phase, src * 2 + core)
-        copy(got, got, fw_s.at[phase, 0], ag_r.at[phase, src], row=sibling).wait_recv()
+        copy(got, got, ag_s.at[phase], ag_r.at[phase, src], row=sibling).wait_recv()
         beyond = pair - toward
         go(
-            phase,
-            copy(got, got, rl_s.at[phase, n], ag_r.at[phase, src], row=lax.rem(beyond + pairs, pairs) * 2 + core),
-            ((apart >= 2) | (beyond == 0) | (beyond == pairs - 1)) & (beyond >= 0) & (beyond < pairs),
+            copy(got, got, rl_s.at[phase], ag_r.at[phase, src], row=lax.rem(beyond + pairs, pairs) * 2 + core),
+            relayed(src, apart, toward),
         )
-        go(phase, copy(got, got, fw_s.at[phase, n + 1], fw_r.at[phase, src], row=sibling))
+        go(copy(got, got, ag_s.at[phase], fw_r.at[phase, src], row=sibling))
 
     def gather_multiply(phase, done):
         before = pair
@@ -257,8 +287,9 @@
             forwarded(phase, before)
             multiply(phase, before, n == 0)
             before = src
+        multiply_half(phase, before * 2 + core, pairs == 1)
         forwarded(phase, before)
-        multiply(phase, before, pairs == 1)
+        multiply_half(phase, before * 2 + 1 - core, False)
         if not dense:
             multiply_sparse(phase)
 
@@ -272,13 +303,12 @@
                 low, high = acc[to, part(q, p), :].astype(BF16), acc[to, part(q, p + 1), :].astype(BF16)
                 stage[phase, to, part(q, p), :] = jnp.where(gone > p, low, high)
             if k:
-                go(phase, copy(stage.at[phase, to, rows_here], landed.at[phase, g, rows_here], rs_s.at[phase, k], rs_r.at[phase, k], grp=to))
+                go(copy(stage.at[phase, to, rows_here], landed.at[phase, g, rows_here], rs_s.at[phase], rs_r.at[phase], grp=to))
 
     def scatter_finish(phase):
         step, q = divmod(phase, CHUNKS)
-        for k in range(1, groups):
-            got = landed.at[phase, partner(k), pl.ds(0, packed[q])]
-            copy(got, got, rs_s.at[phase, k], rs_r.at[phase, k], row=sibling).wait_recv()
+        got = landed.at[phase, pl.ds(0, groups - 1), pl.ds(0, packed[q])]
+        copy(got, got, rs_s.at[phase], rs_r.at[phase], row=sibling).wait_recv()
         gone = tall(q, dgrp[g])
         for p in range(keeps):
             new = stage[phase, g, part(q, p), :].astype(F32)
@@ -328,6 +358,8 @@
     deliver(last_ref, lambda q, p: stage[(STEPS - 1) * CHUNKS + q, g, part(q, p), :])
     for phase in range(phases - 3, phases):
         drain(phase)
+    for k in range(1, groups):
+        copy(dgrp.at[g], dgrp.at[g], dg_s.at[k], dg_r.at[k], row=sibling).wait_send()
 
 
 def per_device(t_start, h_blocks, h_cols, t_cols):
@@ -366,13 +398,12 @@
             pltpu.VMEM((groups, TILE, wide), BF16),
             pltpu.SMEM(h_cols.shape, jnp.int32),
             pltpu.SMEM(t_cols.shape, jnp.int32),
-            dma((phases, 4)),
+            dma((phases,)),
+            dma((phases,)),
+            dma((phases,)),
+            dma((phases,)),
             dma((phases, pairs)),
             dma((phases, pairs)),
-            dma((phases, pairs)),
-            dma((phases, pairs)),
-            dma((phases, groups)),
-            dma((phases, groups)),
             dma((groups,)),
             dma((groups,)),
             dma((4,)),

time: 62.5 us -> 60.4 us (0.966)
  Pallas kernels: 60.3 us -> 58.2 us
    pallas_call x1, Pallas kernels: 60.3 us -> 58.2 us  [per_device(): pl.pallas_call(functools.partial(kernel, (groups, rows, rb, cb, keeps, hr...]
where the time goes in v4:
time: 60.4 us; the launch traced here: 60.3 us
  Pallas kernels  58.2 us (96%)
  local copies, waits for them, and re-layouts  1.41 us (2%)
  between operations  0.64 us (1%)
    pallas_call x1, Pallas kernels, per_device(): pl.pallas_call(functools.partial(kernel, (groups, rows, rb, cb, keeps, hr...  58.2 us
    unnamed x2, local copies, waits for them, and re-layouts  1.41 us

profile of v4, /device:TPU:0, one launch (start us, length us, event | category | flops | bytes accessed | tf_op | source)
XLA Modules:
  0.0 60.3 jit_solution(4829922603717336941)
XLA Ops:
  0.6 58.2 %shard_map.59 = (bf16[256,512]{1,0:T(8,128)(2,1)S(1)}, bf16[256,512]{1,0:T(8,128)(2,1)S(1)}) custom-call(bf16[256,512]{1,0:T(8,128)(2,1)} %t_hbm.1, bf16[8,1,8,128,128]{4,3,2,1,0:T(8,128)(2,1)} %h_hbm.1, s32[8,1,8]{2,1,0:T(1,128)} %hc_hbm.1, s32[2,3]{1,0:T(2,128)} %tc_hbm.1), custom_call_target="tpu_custom_call" | custom-call | tf_op jit(solution)/shard_map/pallas_call | solution.py:377
  58.9 0.7 %copy.8 = bf16[256,512]{1,0:T(8,128)(2,1)} copy(bf16[256,512]{1,0:T(8,128)(2,1)S(1)} %get-tuple-element.2) | data formatting | bytes 524288
  59.6 0.7 %copy.9 = bf16[256,512]{1,0:T(8,128)(2,1)} copy(bf16[256,512]{1,0:T(8,128)(2,1)S(1)} %get-tuple-element.3) | data formatting | bytes 524288

commit v5 on v4

--- a/solution.py
+++ b/solution.py
@@ -36,6 +36,7 @@
     r = lax.axis_index("row")
     pair, core = r // 2, lax.rem(r, 2)
     sibling = pair * 2 + 1 - core
+    home = core * pairs + pair
 
     def part(q, c):
         return slice(c * SIZES[q], (c + 1) * SIZES[q])
@@ -66,10 +67,15 @@
                 other = other + (1 - 2 * lax.rem(g // (1 << i), 2)) * (1 << i)
         return other
 
-    def there(d):
-        if abs(d) == 1:
-            return inside(d)
-        return (pair + d > 0) & (pair + d < pairs - 1)
+    def goals(p):
+        return [p + d for d in reach if (0 <= p + d < pairs if abs(d) == 1 else 0 < p + d < pairs - 1)]
+
+    def pick(values):
+        out = jnp.int32(values[0])
+        if len(set(values)) > 1:
+            for p in range(1, pairs):
+                out = jnp.where(pair == p, values[p], out)
+        return out
 
     def at_pair(d):
         return lax.rem(pair + d + 2 * pairs, pairs) * 2 + core
@@ -100,13 +106,13 @@
         lanes.append(jnp.full((TILE, BS), cb * (cb - 1) // 2 - total, jnp.int32).astype(F32).astype(BF16))
     mark = jnp.concatenate(lanes, axis=1)
     dgrp[g] = mark
-    bufs[0][0, r, full[0] : full[0] + TILE, :] = mark
+    bufs[0][0, home, full[0] : full[0] + TILE, :] = mark
     t_copy.wait()
     turned = tv[...].T
     for q in range(CHUNKS):
         for c in range(cb):
             at = c * BS + FROM[q]
-            bufs[0][q, r, part(q, c), :] = turned[at : at + SIZES[q], :]
+            bufs[0][q, home, part(q, c), :] = turned[at : at + SIZES[q], :]
     pl.semaphore_wait(barrier, greeted)
 
     def go(one, cond=None):
@@ -121,25 +127,34 @@
             return bufs[step].at[q, who, pl.ds(0, packed[q])]
         return bufs[0].at[q, who, pl.ds(0, full[q] + (0 if q else TILE))]
 
-    def gather_start(phase):
-        own = piece(phase, r)
-        for d in reach:
-            go(copy(own, own, ag_s.at[phase], ag_r.at[phase, pair], row=at_pair(d)), there(d))
-        go(copy(own, own, ag_s.at[phase], fw_r.at[phase, pair], row=sibling))
-
     def ranked(p):
         far = 1 if 2 * p < pairs else -1
         short = lambda s: pairs == 4 and (s - p) * far < 0
         return sorted((s for s in range(pairs) if s != p), key=lambda s: (short(s), abs(s - p), (s - p) * far < 0))
 
-    def kth(n):
-        src = jnp.int32(ranked(0)[n])
-        for p in range(1, pairs):
-            src = jnp.where(pair == p, ranked(p)[n], src)
-        toward = jnp.where(src > pair, 1, -1)
-        return src, (src - pair) * toward, toward
-
-    order = [kth(n) for n in range(pairs - 1)]
+    def beyond(p, n):
+        src = ranked(p)[n]
+        to = p + (1 if src < p else -1)
+        return to if 0 <= to < pairs and to not in goals(src) else None
+
+    def counted(lists, k):
+        have = [int(len(one) > k) for one in lists]
+        return None if all(have) else pick(have) == 1
+
+    every = range(pairs)
+    targets = [goals(p) for p in every]
+    sent = [len(one) + pairs for one in targets]
+    onward = [[beyond(p, n) for n in range(pairs - 1)] for p in every]
+    passed = [sum(to is not None for to in one) for one in onward]
+    order = [pick([ranked(p)[n] for p in every]) for n in range(pairs - 1)]
+    early = 2
+
+    def gather_start(phase):
+        own = piece(phase, home)
+        for k in range(max(len(one) for one in targets)):
+            to = pick([one[k] if k < len(one) else one[0] for one in targets])
+            go(copy(own, own, ag_s.at[phase], ag_r.at[phase, pair], row=to * 2 + core), counted(targets, k))
+        go(copy(own, own, ag_s.at[phase], fw_r.at[phase, pair], row=sibling))
 
     for k in range(1, groups):
         go(copy(dgrp.at[g], dgrp.at[g], dg_s.at[k], dg_r.at[k], grp=partner(k)))
@@ -193,32 +208,31 @@
             return bufs[0][q, who, : full[q], :]
         return unpacked(gone_of(q, who), lambda p: bufs[step][q, who, part(q, p), :])
 
-    def multiply_half(phase, who, first):
+    def keep_apart(value, src, n):
+        for b in range(rb):
+            unp[(src * 2 + n) * rb + b, : value.shape[0]] = value[:, b * BS : (b + 1) * BS]
+
+    def accumulate(phase, left, right, first):
         high = full[phase % CHUNKS]
-        if not dense:
-            one = operand(phase, who)
-            for b in range(rb):
-                unp[who * rb + b, :high] = one[:, b * BS : (b + 1) * BS]
-            return
-        right = hd[pl.ds(who * rb, rb)].reshape(wide, hrows * BS)
-        out = jnp.dot(operand(phase, who), right, preferred_element_type=F32)
+        out = jnp.dot(left, right.reshape(left.shape[1], hrows * BS), preferred_element_type=F32)
         for k in range(groups):
             value = out[:, k * wide : (k + 1) * wide]
             acc[k, :high] = value if first else acc[k, :high] + value
 
+    def multiply_half(phase, src, n):
+        one = operand(phase, n * pairs + src)
+        if dense:
+            accumulate(phase, one, hd[pl.ds((src * 2 + n) * rb, rb)], False)
+        else:
+            keep_apart(one, src, n)
+
     def multiply(phase, src, first):
-        both = [operand(phase, src * 2 + n) for n in range(2)]
-        high = full[phase % CHUNKS]
-        if not dense:
+        both = [operand(phase, n * pairs + src) for n in range(2)]
+        if dense:
+            accumulate(phase, jnp.concatenate(both, axis=1), hd[pl.ds(src * 2 * rb, 2 * rb)], first)
+        else:
             for n in range(2):
-                for b in range(rb):
-                    unp[(src * 2 + n) * rb + b, :high] = both[n][:, b * BS : (b + 1) * BS]
-            return
-        right = hd[pl.ds(src * 2 * rb, 2 * rb)].reshape(2 * wide, hrows * BS)
-        out = jnp.dot(jnp.concatenate(both, axis=1), right, preferred_element_type=F32)
-        for k in range(groups):
-            value = out[:, k * wide : (k + 1) * wide]
-            acc[k, :high] = value if first else acc[k, :high] + value
+                keep_apart(both[n], src, n)
 
     def multiply_sparse(phase):
         high = full[phase % CHUNKS]
@@ -237,59 +251,57 @@
         lax.fori_loop(0, groups, one_group, 0)
 
     def forwarded(phase, src):
-        got = piece(phase, src * 2 + 1 - core)
+        got = piece(phase, (1 - core) * pairs + src)
         copy(got, got, ag_s.at[phase], fw_r.at[phase, src], row=sibling).wait_recv()
-
-    def relayed(src, apart, toward):
-        beyond = pair - toward
-        return ((apart >= 2) | (beyond == 0) | (beyond == pairs - 1)) & (beyond >= 0) & (beyond < pairs)
-
-    def total(conds):
-        return sum(jnp.where(cond, 1, 0) for cond in conds)
-
-    sent = total(there(d) for d in reach) + pairs
-    passed = total(relayed(*one) for one in order)
 
     def drain(phase):
         step, q = divmod(phase, CHUNKS)
         high = packed[q] if step else full[q] + (0 if q else TILE)
 
-        def settle(sem, count, choices):
-            for n in choices:
-
-                @pl.when(count == n)
-                def _():
+        def settle(sem, counts):
+            for n in sorted(set(counts) - {0}):
+
+                def wait():
                     some = bufs[step].at[q, pl.ds(0, n), pl.ds(0, high)]
                     copy(some, some, sem.at[phase], sem.at[phase], row=sibling).wait_send()
 
-        few = pairs == 4
-        settle(ag_s, sent, [pairs + 2] if few else range(pairs, pairs + 5))
-        settle(rl_s, passed, [2] if few else range(1, pairs))
+                if len(set(counts)) == 1:
+                    wait()
+                else:
+                    pl.when(pick(counts) == n)(wait)
+
+        settle(ag_s, sent)
+        settle(rl_s, passed)
         some = stage.at[phase, pl.ds(0, groups - 1), pl.ds(0, packed[q])]
         copy(some, some, rs_s.at[phase], rs_s.at[phase], row=sibling).wait_send()
 
     def pass_on(phase, n):
-        src, apart, toward = order[n]
-        got = piece(phase, src * 2 + core)
+        src = order[n]
+        got = piece(phase, core * pairs + src)
         copy(got, got, ag_s.at[phase], ag_r.at[phase, src], row=sibling).wait_recv()
-        beyond = pair - toward
-        go(
-            copy(got, got, rl_s.at[phase], ag_r.at[phase, src], row=lax.rem(beyond + pairs, pairs) * 2 + core),
-            relayed(src, apart, toward),
-        )
+        tos = [one[n] for one in onward]
+        if any(to is not None for to in tos):
+            to = pick([p if to is None else to for p, to in enumerate(tos)])
+            go(
+                copy(got, got, rl_s.at[phase], ag_r.at[phase, src], row=to * 2 + core),
+                None if None not in tos else pick([int(one is not None) for one in tos]) == 1,
+            )
         go(copy(got, got, ag_s.at[phase], fw_r.at[phase, src], row=sibling))
 
-    def gather_multiply(phase, done):
-        before = pair
-        for n, (src, _, _) in enumerate(order):
-            if n >= done:
-                pass_on(phase, n)
-            forwarded(phase, before)
-            multiply(phase, before, n == 0)
-            before = src
-        multiply_half(phase, before * 2 + core, pairs == 1)
-        forwarded(phase, before)
-        multiply_half(phase, before * 2 + 1 - core, False)
+    def gather_multiply(phase):
+        forwarded(phase, pair)
+        multiply(phase, pair, True)
+        last = len(order) - 1
+        for n, src in enumerate(order):
+            if n >= early - 1 and n < last:
+                pass_on(phase, n + 1)
+            if n < last:
+                forwarded(phase, src)
+                multiply(phase, src, False)
+            else:
+                multiply_half(phase, src, core)
+                forwarded(phase, src)
+                multiply_half(phase, src, 1 - core)
         if not dense:
             multiply_sparse(phase)
 
@@ -315,12 +327,12 @@
             for k in range(1, groups):
                 new = new + landed[phase, partner(k), part(q, p), :].astype(F32)
             if step == 1:
-                old = jnp.where(gone > p, bufs[0][q, r, part(q, p), :], bufs[0][q, r, part(q, p + 1), :])
+                old = jnp.where(gone > p, bufs[0][q, home, part(q, p), :], bufs[0][q, home, part(q, p + 1), :])
                 new = 2.0 * new - old.astype(F32)
             elif step > 1:
-                new = 2.0 * new - bufs[step - 1][q, r, part(q, p), :].astype(F32)
+                new = 2.0 * new - bufs[step - 1][q, home, part(q, p), :].astype(F32)
             if step < STEPS - 1:
-                bufs[step + 1][q, r, part(q, p), :] = new.astype(BF16)
+                bufs[step + 1][q, home, part(q, p), :] = new.astype(BF16)
             else:
                 stage[phase, g, part(q, p), :] = new.astype(BF16)
         if step < STEPS - 1:
@@ -331,35 +343,47 @@
         whole = jnp.concatenate([pieces[q][part(q, c), :] for c in range(cb) for q in range(CHUNKS)], axis=0)
         ref[...] = whole.T
 
+    def first_part(phase):
+        for n in range(early):
+            pass_on(phase, n)
+
     turn_blocks()
-    early = min(2, len(order))
-    for n in range(early):
-        pass_on(0, n)
+    first_part(0)
     for q in range(AHEAD, CHUNKS):
         gather_start(q)
     if dense:
         lay_out()
     for phase in range(phases):
-        gather_multiply(phase, early)
+        gather_multiply(phase)
         if phase == 0:
             for k in range(1, groups):
                 got = dgrp.at[partner(k)]
                 copy(got, got, dg_s.at[k], dg_r.at[k], row=sibling).wait_recv()
         scatter_start(phase)
         if phase + 1 < phases:
-            for n in range(early):
-                pass_on(phase + 1, n)
+            first_part(phase + 1)
         if phase:
             scatter_finish(phase - 1)
         if phase >= 3:
             drain(phase - 3)
-    deliver(before_ref, lambda q, p: bufs[STEPS - 1][q, r, part(q, p), :])
+    deliver(before_ref, lambda q, p: bufs[STEPS - 1][q, home, part(q, p), :])
     scatter_finish(phases - 1)
     deliver(last_ref, lambda q, p: stage[(STEPS - 1) * CHUNKS + q, g, part(q, p), :])
     for phase in range(phases - 3, phases):
         drain(phase)
     for k in range(1, groups):
         copy(dgrp.at[g], dgrp.at[g], dg_s.at[k], dg_r.at[k], row=sibling).wait_send()
+
+
+def hand_out(before, last, before_hbm, last_hbm, sems):
+    copies = [
+        pltpu.make_async_copy(before, before_hbm, sems.at[0]),
+        pltpu.make_async_copy(last, last_hbm, sems.at[1]),
+    ]
+    for one in copies:
+        one.start()
+    for one in copies:
+        one.wait()
 
 
 def per_device(t_start, h_blocks, h_cols, t_cols):
@@ -374,7 +398,7 @@
     phases = STEPS * CHUNKS
     dma = pltpu.SemaphoreType.DMA
     out = pltpu.VMEM(t_start.shape, t_start.dtype)
-    return pl.pallas_call(
+    held = pl.pallas_call(
         functools.partial(kernel, (groups, rows, rb, cb, keeps, hrows, slots, dense)),
         out_shape=(out, out),
         in_specs=[
@@ -412,6 +436,15 @@
             collective_id=0, has_side_effects=True, vmem_limit_bytes=56 << 20
         ),
     )(t_start, h_blocks, h_cols, t_cols)
+    out = jax.ShapeDtypeStruct(t_start.shape, t_start.dtype)
+    return pl.pallas_call(
+        hand_out,
+        out_shape=(out, out),
+        in_specs=[pl.BlockSpec(memory_space=pltpu.VMEM)] * 2,
+        out_specs=(pl.BlockSpec(memory_space=pl.ANY),) * 2,
+        scratch_shapes=[dma((2,))],
+        name="hand_out",
+    )(*[pltpu.with_memory_space_constraint(one, pltpu.VMEM) for one in held])
 
 
 def solution(mesh):

time: 60.4 us -> 59.8 us (0.990)
  local copies, waits for them, and re-layouts: 1.41 us -> 0 us
  Pallas kernels: 58.2 us -> 59 us
    unnamed x2 -> x0, local copies, waits for them, and re-layouts: 1.41 us -> none
    pallas_call x0 -> x1, Pallas kernels: none -> 0.81 us  [per_device(): pl.pallas_call(hand_out, out_shape=(out, out), in_specs=[pl.BlockSpec(mem...]
where the time goes in v5:
time: 59.8 us; the launch traced here: 59.7 us
  Pallas kernels  59 us (99%)
  between operations  0.64 us (1%)
    pallas_call x1, Pallas kernels, per_device(): pl.pallas_call(functools.partial(kernel, (groups, rows, rb, cb, keeps, hr...  58.2 us

profile of v5, /device:TPU:0, one launch (start us, length us, event | category | flops | bytes accessed | tf_op | source)
XLA Modules:
  0.0 59.7 jit_solution(17868054785829982198)
XLA Ops:
  0.6 58.2 %shard_map.59 = (bf16[256,512]{1,0:T(8,128)(2,1)S(1)}, bf16[256,512]{1,0:T(8,128)(2,1)S(1)}) custom-call(bf16[256,512]{1,0:T(8,128)(2,1)} %t_hbm.1, bf16[8,1,8,128,128]{4,3,2,1,0:T(8,128)(2,1)} %h_hbm.1, s32[8,1,8]{2,1,0:T(1,128)} %hc_hbm.1, s32[2,3]{1,0:T(2,128)} %tc_hbm.1), custom_call_target="tpu_custom_call" | custom-call | tf_op jit(solution)/shard_map/pallas_call | solution.py:401
  58.9 0.8 %hand_out.1 = (bf16[256,512]{1,0:T(8,128)(2,1)}, bf16[256,512]{1,0:T(8,128)(2,1)}) custom-call(bf16[256,512]{1,0:T(8,128)(2,1)S(1)} %get-tuple-element.4.before, bf16[256,512]{1,0:T(8,128)(2,1)S(1)} %get-tuple-element.5.last), custom_call_target="tpu_custom_call" | custom-call | tf_op jit(solution)/shard_map/hand_out/pallas_call | solution.py:440

commit v6 on v5

--- a/solution.py
+++ b/solution.py
@@ -106,7 +106,7 @@
         lanes.append(jnp.full((TILE, BS), cb * (cb - 1) // 2 - total, jnp.int32).astype(F32).astype(BF16))
     mark = jnp.concatenate(lanes, axis=1)
     dgrp[g] = mark
-    bufs[0][0, home, full[0] : full[0] + TILE, :] = mark
+    bufs[0][CHUNKS - 1, home, full[-1] : full[-1] + TILE, :] = mark
     t_copy.wait()
     turned = tv[...].T
     for q in range(CHUNKS):
@@ -125,7 +125,7 @@
         step, q = divmod(phase, CHUNKS)
         if step:
             return bufs[step].at[q, who, pl.ds(0, packed[q])]
-        return bufs[0].at[q, who, pl.ds(0, full[q] + (0 if q else TILE))]
+        return bufs[0].at[q, who, pl.ds(0, full[q] + (TILE if q == CHUNKS - 1 else 0))]
 
     def ranked(p):
         far = 1 if 2 * p < pairs else -1
@@ -187,7 +187,7 @@
         return jnp.concatenate([tile] * (SIZES[q] // TILE), axis=0)
 
     def gone_of(q, who):
-        return tall(q, bufs[0][0, who, full[0] : full[0] + TILE, :])
+        return tall(q, bufs[0][CHUNKS - 1, who, full[-1] : full[-1] + TILE, :])
 
     def unpacked(gone, value):
         zero = jnp.zeros(gone.shape, BF16)
@@ -256,7 +256,7 @@
 
     def drain(phase):
         step, q = divmod(phase, CHUNKS)
-        high = packed[q] if step else full[q] + (0 if q else TILE)
+        high = packed[q] if step else full[q] + (TILE if q == CHUNKS - 1 else 0)
 
         def settle(sem, counts):
             for n in sorted(set(counts) - {0}):

time: 59.8 us -> 59.8 us (level)
  no operation moved by 1% of the time
where the time goes in v6:
time: 59.8 us; the launch traced here: 59.7 us
  Pallas kernels  59 us (99%)
  between operations  0.64 us (1%)
    pallas_call x1, Pallas kernels, per_device(): pl.pallas_call(functools.partial(kernel, (groups, rows, rb, cb, keeps, hr...  58.2 us

profile of v6, /device:TPU:0, one launch (start us, length us, event | category | flops | bytes accessed | tf_op | source)
XLA Modules:
  0.0 59.7 jit_solution(2207743332605979202)
XLA Ops:
  0.6 58.2 %shard_map.59 = (bf16[256,512]{1,0:T(8,128)(2,1)S(1)}, bf16[256,512]{1,0:T(8,128)(2,1)S(1)}) custom-call(bf16[256,512]{1,0:T(8,128)(2,1)} %t_hbm.1, bf16[8,1,8,128,128]{4,3,2,1,0:T(8,128)(2,1)} %h_hbm.1, s32[8,1,8]{2,1,0:T(1,128)} %hc_hbm.1, s32[2,3]{1,0:T(2,128)} %tc_hbm.1), custom_call_target="tpu_custom_call" | custom-call | tf_op jit(solution)/shard_map/pallas_call | solution.py:401
  58.9 0.8 %hand_out.1 = (bf16[256,512]{1,0:T(8,128)(2,1)}, bf16[256,512]{1,0:T(8,128)(2,1)}) custom-call(bf16[256,512]{1,0:T(8,128)(2,1)S(1)} %get-tuple-element.4.before, bf16[256,512]{1,0:T(8,128)(2,1)S(1)} %get-tuple-element.5.last), custom_call_target="tpu_custom_call" | custom-call | tf_op jit(solution)/shard_map/hand_out/pallas_call | solution.py:440
